TPU v7x, 32 devices: a whole 2x2x4 slice. The times are simulated.
32 devices in a mesh: section: 16 (over z, y, x), head: 2 (over core).
Axes of the slice: x: 2, y: 2, z: 4, core: 2. Of those that a mesh axis runs over, the one named last changes fastest.
Arguments:
- queries: bfloat16 [3072, 1024], P('section', 'head'), may hold values from -20 to 20
- keys: bfloat16 [3072, 256], P('section', 'head'), may hold values from -20 to 20
- values: bfloat16 [3072, 256], P('section', 'head'), may hold values from -6 to 6
- d_attn: bfloat16 [3072, 1024], P('section', 'head'), may hold values from -72 to 72
- d_out: bfloat16 [3072, 4096], P('section', 'head'), may hold values from -6 to 6
- w_query: bfloat16 [4096, 1024], P(None, 'head'), may hold values from -0.09375 to 0.09375
- prefix_len: int32 [16], replicated, may hold values from 0 to 2880, as said below
Outputs:
- grad_prev: bfloat16 [3072, 4096], P('section', 'head')
Inputs may be any that keep to these rules, and one draw needn't show every extreme that they name: prefix_len[s] <= s * 192 for every slice s; the first slice's is 0 and the last slice's is 2880.
All inputs are finite; a program needn't handle non-finite values.
Results may differ from a plain program's by a relative error of at most 0.035.
Values may be sent and summed in bfloat16 or wider, within the bound.
A program may use at most 64 MiB of HBM per device.

v0:
```python
import jax
import jax.numpy as jnp
from jax import lax
from jax.sharding import PartitionSpec as P

masked_score = -1e30
key_block = 512


def shifted(value, axis, steps):
    count = lax.axis_size(axis)
    first, last = (max(0, -steps), min(count, count - steps))
    return lax.ppermute(value, axis, [(source, source + steps) for source in range(first, last)])


def head_rows(matrix, head_count):
    row_count = matrix.shape[0]
    head_width = matrix.shape[1] // head_count
    return (
        matrix.reshape(row_count, head_count, head_width)
        .transpose(1, 0, 2)
        .reshape(head_count * row_count, head_width)
    )


def row_heads(matrix, head_count):
    row_count = matrix.shape[0] // head_count
    head_width = matrix.shape[1]
    return (
        matrix.reshape(head_count, row_count, head_width)
        .transpose(1, 0, 2)
        .reshape(row_count, head_count * head_width)
    )


def empty_state(slot_count, head_width):
    return (
        jnp.full((slot_count,), masked_score, jnp.float32),
        jnp.zeros((slot_count,), jnp.float32),
        jnp.zeros((slot_count,), jnp.float32),
        jnp.zeros((slot_count, head_width), jnp.float32),
        jnp.zeros((slot_count, head_width), jnp.float32),
    )


def absorb(running, query_set, key_part, value_part, first_key):
    query_rows, grad_rows, positions, lower_key, upper_key = query_set
    run_max, run_sum, run_delta, total_grad, total_key = running
    key_count = key_part.shape[0]
    key_position = first_key + jnp.arange(key_count, dtype=jnp.int32)
    allowed = (
        (key_position[None, :] >= lower_key)
        & (key_position[None, :] < upper_key)
        & (key_position[None, :] <= positions[:, None])
    )
    scores = lax.dot_general(
        query_rows, key_part, (((1,), (1,)), ((), ())), preferred_element_type=jnp.float32
    ) * query_rows.shape[1] ** (-0.5)
    scores = jnp.where(allowed, scores, masked_score)
    new_max = jnp.maximum(run_max, jnp.max(scores, axis=1))
    factor = jnp.exp(run_max - new_max)
    weights = jnp.where(allowed, jnp.exp(scores - new_max[:, None]), 0.0)
    grad_prob = lax.dot_general(
        grad_rows, value_part, (((1,), (1,)), ((), ())), preferred_element_type=jnp.float32
    )
    weighted = weights * grad_prob
    run_sum = run_sum * factor + jnp.sum(weights, axis=1)
    run_delta = run_delta * factor + jnp.sum(weighted, axis=1)
    total_grad = total_grad * factor[:, None] + jnp.dot(
        weighted.astype(jnp.bfloat16), key_part, preferred_element_type=jnp.float32
    )
    total_key = total_key * factor[:, None] + jnp.dot(
        weights.astype(jnp.bfloat16), key_part, preferred_element_type=jnp.float32
    )
    return (new_max, run_sum, run_delta, total_grad, total_key)


def sweep_keys(running, query_set, portion, anchor):
    piece_rows = portion.shape[0]
    block_count = (piece_rows + key_block - 1) // key_block
    head_width = portion.shape[1] // 2
    lower_key = query_set[3]
    upper_key = jnp.minimum(query_set[4], anchor + piece_rows)
    clipped_set = (query_set[0], query_set[1], query_set[2], lower_key, upper_key)

    def visit_block(turn_index, held):
        offset = turn_index * key_block
        sub_block = lax.dynamic_slice_in_dim(portion, offset, key_block, 0)
        within = (offset + key_block > lower_key) & (offset < upper_key)
        return lax.cond(
            within,
            lambda inner: absorb(
                inner, clipped_set, sub_block[:, :head_width], sub_block[:, head_width:], offset
            ),
            lambda inner: inner,
            held,
        )

    return lax.fori_loop(0, block_count, visit_block, running)


def shards(queries, keys, values, d_attn, d_out, w_query, prefix_len):
    row_count = queries.shape[0]
    head_width = keys.shape[1]
    head_count = queries.shape[1] // head_width
    slot_count = head_count * row_count
    section_count = lax.axis_size("section")
    section_id = lax.axis_index("section")
    key_values = jnp.concatenate([keys, values], axis=1)
    base_row = section_id * row_count
    positions = jnp.tile(base_row + jnp.arange(row_count, dtype=jnp.int32), head_count)
    lower_key = jnp.maximum(base_row - prefix_len[section_id], 0)
    upper_key = jnp.minimum(base_row + row_count, section_count * row_count)
    own_set = (
        head_rows(queries, head_count),
        head_rows(d_attn, head_count),
        positions,
        lower_key,
        upper_key,
    )
    attention_state = sweep_keys(
        empty_state(slot_count, head_width),
        own_set,
        lax.all_gather(key_values, "section", axis=0, tiled=True),
        jnp.int32(0),
    )
    run_max, run_sum, run_delta, total_grad, total_key = attention_state
    delta_rows = run_delta / run_sum
    query_grad = (
        (total_grad - delta_rows[:, None] * total_key) / run_sum[:, None] * head_width ** (-0.5)
    )
    grad_query = row_heads(query_grad, head_count).astype(jnp.bfloat16)
    summed = lax.psum_scatter(
        lax.dot_general(
            w_query, grad_query, (((1,), (1,)), ((), ())), preferred_element_type=jnp.float32
        ).astype(jnp.bfloat16),
        "head",
        scatter_dimension=0,
        tiled=True,
    ).astype(jnp.float32)
    hidden = (d_out.astype(jnp.float32) + summed.T).astype(jnp.bfloat16)
    return shifted(hidden, "section", -1)


def solution(mesh):
    placed = (
        P("section", "head"),
        P("section", "head"),
        P("section", "head"),
        P("section", "head"),
        P("section", "head"),
        P(None, "head"),
        P(),
    )
    return jax.shard_map(
        shards, mesh=mesh, in_specs=placed, out_specs=P("section", "head"), check_vma=False
    )
```

profile of v0, /device:TPU:25, one launch (start us, length us, event | category | flops | bytes accessed | tf_op | source)
XLA Modules:
  0.0 155.2 jit_solution(5692403306449211908)
XLA Ops:
  6.5 1.5 pad_maximum_fusion
  11.2 54.7 %all-gather.2.cloned.1.call-done = bf16[3072,256]{1,0:T(8,128)(2,1)} async-done(((bf16[192,256]{1,0:T(8,128)(2,1)}), bf16[3072,256]{1,0:T(8,128)(2,1)}) %all-gather.2.cloned.1.call-update) | async-done | bytes 1572880 | tf_op jit(solution)/shard_map/all_gather | solution.py:124
  65.9 35.2 %while.22 = (s32[]{:T(128)}, f32[768]{0:T(1024)S(1)}, f32[768]{0:T(1024)S(1)}, f32[768]{0:T(1024)S(1)}, f32[768,128]{1,0:T(8,128)S(1)}, /*index=5*/f32[768,128]{...) while((s32[]{:T(128)}, f32[768]{0:T(1024)S(1)}, ...), condition=%wide.region_6.7_spmd.clone, body=%wide.region_0.6_spmd.clone.sunk | while | flops 411702016 | bytes 10460873 | solution.py:99
  66.0 7.0 %conditional.3 = ((f32[768]{0:T(1024)S(1)}, f32[768]{0:T(1024)S(1)}, f32[768]{0:T(1024)S(1)}, f32[768,128]{1,0:T(8,128)S(1)}, f32[768,128]{1,0:T(8,128)S(1)})) conditional(s32[]{:T(128)} %convert_element_type.62, (f32[768]{0:T(1024)S(1)}, f32[768]{0:T(1024)S(1)}, f32[768]{0:T(1024)S(1)}, f32[768,128]{1,0:T(8,128)S(1)}, ...), branch_computations={%region_1.0_spmd, %region_2.5_spmd} | conditional | flops 411702016 | bytes 10460546 | solution.py:90
  67.5 1.6 %fusion.17 = (f32[768]{0:T(1024)S(1)}, bf16[768,512]{0,1:T(8,128)(2,1)S(1)}) fusion(bf16[768,128]{1,0:T(8,128)(2,1)S(1)} %get-tuple-element.313, bf16[3072,256]{1,0:T(8,128)(2,1)} %get-tuple-element.309, s32[]{:T(128)S(6)} %select_n.20, s32[]{:T(128)S(6)} %add.96, f32[768,512]{0,1:T(8,128)S(1)} %get-tuple-element.402, f32[768]{0:T(1024)S(1)} %max.6, ...), kind=kOutput, calls=%fused_computation.34 | convolution fusion | flops 103415040 | bytes 2698760 | tf_op jit(solution)/shard_map/while/body/eval_jaxpr/cond/branch_1_fun/dot_general | solution.py:63
  69.7 1.5 convolution_add_fusion.1
  71.2 1.7 %convolution_add_fusion = f32[768,128]{1,0:T(8,128)S(1)} fusion(f32[768,128]{1,0:T(8,128)S(1)} %get-tuple-element.315, f32[768]{0:T(1024)S(1)} %get-tuple-element.400, bf16[3072,256]{1,0:T(8,128)(2,1)} %get-tuple-element.309, s32[]{:T(128)S(6)} %select_n.20, f32[768,512]{0,1:T(8,128)S(1)} %get-tuple-element.402, f32[768]{0:T(1024)S(1)} %max.6, ...), kind=kOutput, calls=%fused_computation.5 | convolution fusion | flops 102825984 | bytes 2502148 | tf_op jit(solution)/shard_map/while/body/eval_jaxpr/cond/branch_1_fun/dot_general | solution.py:72
  73.0 7.0 %conditional.3 = ((f32[768]{0:T(1024)S(1)}, f32[768]{0:T(1024)S(1)}, f32[768]{0:T(1024)S(1)}, f32[768,128]{1,0:T(8,128)S(1)}, f32[768,128]{1,0:T(8,128)S(1)})) conditional(s32[]{:T(128)} %convert_element_type.62, (f32[768]{0:T(1024)S(1)}, f32[768]{0:T(1024)S(1)}, f32[768]{0:T(1024)S(1)}, f32[768,128]{1,0:T(8,128)S(1)}, ...), branch_computations={%region_1.0_spmd, %region_2.5_spmd} | conditional | flops 411702016 | bytes 10460546 | solution.py:90
  74.6 1.6 %fusion.17 = (f32[768]{0:T(1024)S(1)}, bf16[768,512]{0,1:T(8,128)(2,1)S(1)}) fusion(bf16[768,128]{1,0:T(8,128)(2,1)S(1)} %get-tuple-element.313, bf16[3072,256]{1,0:T(8,128)(2,1)} %get-tuple-element.309, s32[]{:T(128)S(6)} %select_n.20, s32[]{:T(128)S(6)} %add.96, f32[768,512]{0,1:T(8,128)S(1)} %get-tuple-element.402, f32[768]{0:T(1024)S(1)} %max.6, ...), kind=kOutput, calls=%fused_computation.34 | convolution fusion | flops 103415040 | bytes 2698760 | tf_op jit(solution)/shard_map/while/body/eval_jaxpr/cond/branch_1_fun/dot_general | solution.py:63
  78.2 1.7 %convolution_add_fusion = f32[768,128]{1,0:T(8,128)S(1)} fusion(f32[768,128]{1,0:T(8,128)S(1)} %get-tuple-element.315, f32[768]{0:T(1024)S(1)} %get-tuple-element.400, bf16[3072,256]{1,0:T(8,128)(2,1)} %get-tuple-element.309, s32[]{:T(128)S(6)} %select_n.20, f32[768,512]{0,1:T(8,128)S(1)} %get-tuple-element.402, f32[768]{0:T(1024)S(1)} %max.6, ...), kind=kOutput, calls=%fused_computation.5 | convolution fusion | flops 102825984 | bytes 2502148 | tf_op jit(solution)/shard_map/while/body/eval_jaxpr/cond/branch_1_fun/dot_general | solution.py:72
  80.0 7.0 %conditional.3 = ((f32[768]{0:T(1024)S(1)}, f32[768]{0:T(1024)S(1)}, f32[768]{0:T(1024)S(1)}, f32[768,128]{1,0:T(8,128)S(1)}, f32[768,128]{1,0:T(8,128)S(1)})) conditional(s32[]{:T(128)} %convert_element_type.62, (f32[768]{0:T(1024)S(1)}, f32[768]{0:T(1024)S(1)}, f32[768]{0:T(1024)S(1)}, f32[768,128]{1,0:T(8,128)S(1)}, ...), branch_computations={%region_1.0_spmd, %region_2.5_spmd} | conditional | flops 411702016 | bytes 10460546 | solution.py:90
  81.6 1.6 %fusion.17 = (f32[768]{0:T(1024)S(1)}, bf16[768,512]{0,1:T(8,128)(2,1)S(1)}) fusion(bf16[768,128]{1,0:T(8,128)(2,1)S(1)} %get-tuple-element.313, bf16[3072,256]{1,0:T(8,128)(2,1)} %get-tuple-element.309, s32[]{:T(128)S(6)} %select_n.20, s32[]{:T(128)S(6)} %add.96, f32[768,512]{0,1:T(8,128)S(1)} %get-tuple-element.402, f32[768]{0:T(1024)S(1)} %max.6, ...), kind=kOutput, calls=%fused_computation.34 | convolution fusion | flops 103415040 | bytes 2698760 | tf_op jit(solution)/shard_map/while/body/eval_jaxpr/cond/branch_1_fun/dot_general | solution.py:63
  83.7 1.5 convolution_add_fusion.1
  85.2 1.7 %convolution_add_fusion = f32[768,128]{1,0:T(8,128)S(1)} fusion(f32[768,128]{1,0:T(8,128)S(1)} %get-tuple-element.315, f32[768]{0:T(1024)S(1)} %get-tuple-element.400, bf16[3072,256]{1,0:T(8,128)(2,1)} %get-tuple-element.309, s32[]{:T(128)S(6)} %select_n.20, f32[768,512]{0,1:T(8,128)S(1)} %get-tuple-element.402, f32[768]{0:T(1024)S(1)} %max.6, ...), kind=kOutput, calls=%fused_computation.5 | convolution fusion | flops 102825984 | bytes 2502148 | tf_op jit(solution)/shard_map/while/body/eval_jaxpr/cond/branch_1_fun/dot_general | solution.py:72
  87.0 7.0 %conditional.3 = ((f32[768]{0:T(1024)S(1)}, f32[768]{0:T(1024)S(1)}, f32[768]{0:T(1024)S(1)}, f32[768,128]{1,0:T(8,128)S(1)}, f32[768,128]{1,0:T(8,128)S(1)})) conditional(s32[]{:T(128)} %convert_element_type.62, (f32[768]{0:T(1024)S(1)}, f32[768]{0:T(1024)S(1)}, f32[768]{0:T(1024)S(1)}, f32[768,128]{1,0:T(8,128)S(1)}, ...), branch_computations={%region_1.0_spmd, %region_2.5_spmd} | conditional | flops 411702016 | bytes 10460546 | solution.py:90
  88.6 1.6 %fusion.17 = (f32[768]{0:T(1024)S(1)}, bf16[768,512]{0,1:T(8,128)(2,1)S(1)}) fusion(bf16[768,128]{1,0:T(8,128)(2,1)S(1)} %get-tuple-element.313, bf16[3072,256]{1,0:T(8,128)(2,1)} %get-tuple-element.309, s32[]{:T(128)S(6)} %select_n.20, s32[]{:T(128)S(6)} %add.96, f32[768,512]{0,1:T(8,128)S(1)} %get-tuple-element.402, f32[768]{0:T(1024)S(1)} %max.6, ...), kind=kOutput, calls=%fused_computation.34 | convolution fusion | flops 103415040 | bytes 2698760 | tf_op jit(solution)/shard_map/while/body/eval_jaxpr/cond/branch_1_fun/dot_general | solution.py:63
  92.3 1.7 %convolution_add_fusion = f32[768,128]{1,0:T(8,128)S(1)} fusion(f32[768,128]{1,0:T(8,128)S(1)} %get-tuple-element.315, f32[768]{0:T(1024)S(1)} %get-tuple-element.400, bf16[3072,256]{1,0:T(8,128)(2,1)} %get-tuple-element.309, s32[]{:T(128)S(6)} %select_n.20, f32[768,512]{0,1:T(8,128)S(1)} %get-tuple-element.402, f32[768]{0:T(1024)S(1)} %max.6, ...), kind=kOutput, calls=%fused_computation.5 | convolution fusion | flops 102825984 | bytes 2502148 | tf_op jit(solution)/shard_map/while/body/eval_jaxpr/cond/branch_1_fun/dot_general | solution.py:72
  94.1 7.0 %conditional.3 = ((f32[768]{0:T(1024)S(1)}, f32[768]{0:T(1024)S(1)}, f32[768]{0:T(1024)S(1)}, f32[768,128]{1,0:T(8,128)S(1)}, f32[768,128]{1,0:T(8,128)S(1)})) conditional(s32[]{:T(128)} %convert_element_type.62, (f32[768]{0:T(1024)S(1)}, f32[768]{0:T(1024)S(1)}, f32[768]{0:T(1024)S(1)}, f32[768,128]{1,0:T(8,128)S(1)}, ...), branch_computations={%region_1.0_spmd, %region_2.5_spmd} | conditional | flops 411702016 | bytes 10460546 | solution.py:90
  95.6 1.6 %fusion.17 = (f32[768]{0:T(1024)S(1)}, bf16[768,512]{0,1:T(8,128)(2,1)S(1)}) fusion(bf16[768,128]{1,0:T(8,128)(2,1)S(1)} %get-tuple-element.313, bf16[3072,256]{1,0:T(8,128)(2,1)} %get-tuple-element.309, s32[]{:T(128)S(6)} %select_n.20, s32[]{:T(128)S(6)} %add.96, f32[768,512]{0,1:T(8,128)S(1)} %get-tuple-element.402, f32[768]{0:T(1024)S(1)} %max.6, ...), kind=kOutput, calls=%fused_computation.34 | convolution fusion | flops 103415040 | bytes 2698760 | tf_op jit(solution)/shard_map/while/body/eval_jaxpr/cond/branch_1_fun/dot_general | solution.py:63
  99.3 1.7 %convolution_add_fusion = f32[768,128]{1,0:T(8,128)S(1)} fusion(f32[768,128]{1,0:T(8,128)S(1)} %get-tuple-element.315, f32[768]{0:T(1024)S(1)} %get-tuple-element.400, bf16[3072,256]{1,0:T(8,128)(2,1)} %get-tuple-element.309, s32[]{:T(128)S(6)} %select_n.20, f32[768,512]{0,1:T(8,128)S(1)} %get-tuple-element.402, f32[768]{0:T(1024)S(1)} %max.6, ...), kind=kOutput, calls=%fused_computation.5 | convolution fusion | flops 102825984 | bytes 2502148 | tf_op jit(solution)/shard_map/while/body/eval_jaxpr/cond/branch_1_fun/dot_general | solution.py:72
  101.6 4.9 %fusion.12 = bf16[4096,192]{0,1:T(8,128)(2,1)} fusion(bf16[4096,512]{1,0:T(8,128)(2,1)} %param.16, bf16[24,8,4,128]{3,2,1,0:T(4,128)(2,1)S(1)} %bitcast.37), kind=kOutput, calls=%fused_computation.23 | convolution fusion | flops 806092800 | bytes 5963776 | tf_op jit(solution)/shard_map/dot_general | solution.py:134
  106.5 18.8 %reduce-scatter.2.cloned.1.call-done = bf16[2048,192]{0,1:T(8,128)(2,1)} async-done(((bf16[4096,192]{0,1:T(8,128)(2,1)}), bf16[2048,192]{0,1:T(8,128)(2,1)}) %reduce-scatter.2.cloned.1.call-update) | async-done | bytes 786448 | tf_op jit(solution)/shard_map/reduce_scatter | solution.py:133
  126.7 4.0 %collective-permute-start = (bf16[192,2048]{1,0:T(8,128)(2,1)S(1)}, bf16[192,2048]{1,0:T(8,128)(2,1)S(1)}, u32[]{:S(2)}, u32[]{:S(2)}) collective-permute-start(bf16[192,2048]{1,0:T(8,128)(2,1)S(1)} %fusion.13), channel_id=1, source_target_pairs={{2,0},{4,2},{6,4},{8,6},{10,8},{12,10},{14,12},{16,14},{18,16},{20... | collective-permute-start | bytes 2359304 | tf_op jit(solution)/shard_map/ppermute | solution.py:13
  130.6 16.8 %collective-permute-done = bf16[192,2048]{1,0:T(8,128)(2,1)S(1)} collective-permute-done((bf16[192,2048]{1,0:T(8,128)(2,1)S(1)}, bf16[192,2048]{1,0:T(8,128)(2,1)S(1)}, u32[]{:S(2)}, u32[]{:S(2)}) %collective-permute-start) | collective-permute-done | bytes 786464 | tf_op jit(solution)/shard_map/ppermute | solution.py:13
  (76 shorter events, 20.0 us)
Async XLA Ops:
  6.5 3.6 %copy-start = (bf16[192,512]{1,0:T(8,128)(2,1)S(1)}, bf16[192,512]{1,0:T(8,128)(2,1)}, u32[]{:S(2)}) copy-start(bf16[192,512]{1,0:T(8,128)(2,1)} %param.11) | copy-start | bytes 589828
  6.5 59.3 %all-gather.2.cloned.1.call-start = ((), (), s32[]{:S(2)}) async-start(), calls=%async_computation.1 | async-start | bytes 1671168 | tf_op jit(solution)/shard_map/all_gather | solution.py:124
  8.1 117.2 %reduce-scatter.2.cloned.1.call-start = ((), (), s32[]{:S(2)}) async-start(), calls=%async_computation.2 | async-start | bytes 2359296 | tf_op jit(solution)/shard_map/reduce_scatter | solution.py:133
  106.4 18.8 %copy-start.1 = (bf16[192,2048]{1,0:T(8,128)(2,1)S(1)}, bf16[192,2048]{1,0:T(8,128)(2,1)}, u32[]{:S(2)}) copy-start(bf16[192,2048]{1,0:T(8,128)(2,1)} %param.15) | copy-start | bytes 2359300
  126.7 20.8 %collective-permute-start = (bf16[192,2048]{1,0:T(8,128)(2,1)S(1)}, bf16[192,2048]{1,0:T(8,128)(2,1)S(1)}, u32[]{:S(2)}, u32[]{:S(2)}) collective-permute-start(bf16[192,2048]{1,0:T(8,128)(2,1)S(1)} %fusion.13), channel_id=1, source_target_pairs={{2,0},{4,2},{6,4},{8,6},{10,8},{12,10},{14,12},{16,14},{18,16},{20... | collective-permute-start | bytes 2359304 | tf_op jit(solution)/shard_map/ppermute | solution.py:13
Sparse Core Ops, SparseCore 0:
  10.1 55.6 all-gather.1
  106.6 18.6 reduce-scatter.1
where the time goes:
time: 158 us; the launch traced here: 155 us
  waiting for transfers between devices  90.3 us (57%)
  matrix products  36.2 us (23%)
  between operations  14.2 us (9%)
  other arithmetic  5.85 us (4%)
  starting transfers between devices  4.02 us (3%)
  local copies, waits for them, and re-layouts  3.84 us (2%)
    all_gather x1, waiting for transfers between devices, shards(): lax.all_gather(key_values, 'section', axis=0, tiled=True)  54.7 us
    reduce_scatter x1, waiting for transfers between devices, shards(): lax.psum_scatter(lax.dot_general(w_query, grad_query, (((1,), (1,)), ((),...  18.8 us
    ppermute x1, waiting for transfers between devices, shifted(): lax.ppermute(value, axis, [(source, source + steps) for source in range(f...  16.8 us
    dot_general x5, matrix products, absorb(): jnp.dot(weights.astype(jnp.bfloat16), key_part, preferred_element_type=jn...  8.7 us
    dot_general x5, matrix products, absorb(): lax.dot_general(grad_rows, value_part, (((1,), (1,)), ((), ())), preferre...  7.91 us
    dot_general x5, matrix products, absorb(): jnp.dot(weighted.astype(jnp.bfloat16), key_part, preferred_element_type=j...  7.54 us
    dot_general x5, matrix products, absorb(): lax.dot_general(query_rows, key_part, (((1,), (1,)), ((), ())), preferred...  7.2 us
    dot_general x1, matrix products, shards(): lax.dot_general(w_query, grad_query, (((1,), (1,)), ((), ())), preferred_...  4.88 us
  transfers between devices with their start and end apart: 3, of which 3 were waited for; matrix products, arithmetic and copies ran while one was open for 1% of the time, Pallas kernels for 0%

commit v1 on v0

v1 whole, which is shorter than its diff:
```python
import functools

import jax
import jax.numpy as jnp
from jax import lax
from jax.experimental import pallas as pl
from jax.experimental.pallas import tpu as pltpu
from jax.sharding import PartitionSpec as P

MESH = pl.DeviceIdType.MESH
masked_score = -1e30
log2_e = 1.4426950408889634
plane = 4
near_planes = 2
proj_tile = 512


def rows_by_rows(left, right):
    return lax.dot_general(
        left, right, (((1,), (1,)), ((), ())), preferred_element_type=jnp.float32
    )


def kernel(
    sections, heads, prefix_ref, q_ref, k_ref, v_ref, g_ref, dout_ref, w_ref, out_ref,
    kv, mine, gq, wbuf, din, run_max, run_sum, run_delta, total_grad, total_key,
    kv_recv, x_send, y_send, z_send, w_send, w_recv, w_local, d_send, d_recv,
    gq_send, gq_recv, fan_send, fan_recv,
):
    s = lax.axis_index("section")
    h = lax.axis_index("head")
    rows, head_width = k_ref.shape
    head_count = q_ref.shape[1] // head_width
    features = dout_ref.shape[1]
    planes = sections // plane
    z = s // plane
    p = s % plane
    x = p % 2
    y = p // 2
    px = p + 1 - 2 * x
    py = p + 2 - 4 * y
    pd = px + 2 - 4 * y
    x_side = z * plane + px
    y_side = z * plane + py

    def block(b):
        return kv.at[pl.ds(pl.multiple_of(b * rows, rows), rows), :]

    def kv_copy(b, target, sends):
        return pltpu.make_async_remote_copy(
            src_ref=block(b), dst_ref=block(b), send_sem=sends.at[b], recv_sem=kv_recv.at[b],
            device_id=(target, h), device_id_type=MESH,
        )

    def to_x(b):
        return kv_copy(b, x_side, x_send)

    def to_y(b):
        return kv_copy(b, y_side, y_send)

    def to_z(b):
        return kv_copy(b, s + plane, z_send)

    def arrive(b):
        to_x(b).wait_recv()

    barrier = pltpu.get_barrier_semaphore()

    def greet(section, head):
        pl.semaphore_signal(barrier, inc=1, device_id=(section, head), device_id_type=MESH)

    up = (z < planes - 1).astype(jnp.int32)
    down = (z > 0).astype(jnp.int32)
    after = (s < sections - 1).astype(jnp.int32)
    before = (s > 0).astype(jnp.int32)
    greet(x_side, h)
    greet(y_side, h)
    for step in range(1, heads):
        greet(s, (h + step) % heads)

    @pl.when(z < planes - 1)
    def _():
        greet(s + plane, h)

    @pl.when(z > 0)
    def _():
        greet(s - plane, h)

    @pl.when(s < sections - 1)
    def _():
        greet(s + 1, h)

    @pl.when(s > 0)
    def _():
        greet(s - 1, h)

    kv[pl.ds(pl.multiple_of(s * rows, rows), rows), :head_width] = k_ref[...]
    kv[pl.ds(pl.multiple_of(s * rows, rows), rows), head_width:] = v_ref[...]
    pl.semaphore_wait(barrier, 1 + heads + up + down + after + before)

    to_x(s).start()
    to_y(s).start()

    @pl.when(z < planes - 1)
    def _():
        to_z(s).start()

    def w_copy(step):
        peer = (h + step) % heads
        return pltpu.make_async_remote_copy(
            src_ref=w_ref.at[pl.ds(pl.multiple_of(peer * features, features), features), :],
            dst_ref=wbuf.at[h], send_sem=w_send.at[step], recv_sem=w_recv.at[step],
            device_id=(s, peer), device_id_type=MESH,
        )

    own_w = pltpu.make_async_copy(
        w_ref.at[pl.ds(pl.multiple_of(h * features, features), features), :], wbuf.at[h], w_local
    )

    def w_arrive(step):
        sender = (h + heads - step) % heads
        pltpu.make_async_remote_copy(
            src_ref=wbuf.at[sender], dst_ref=wbuf.at[sender],
            send_sem=w_send.at[step], recv_sem=w_recv.at[step],
            device_id=(s, sender), device_id_type=MESH,
        ).wait_recv()

    d_copy = pltpu.make_async_remote_copy(
        src_ref=dout_ref, dst_ref=din, send_sem=d_send, recv_sem=d_recv,
        device_id=(s - 1, h), device_id_type=MESH,
    )
    gq_copy = pltpu.make_async_remote_copy(
        src_ref=mine, dst_ref=gq.at[h], send_sem=gq_send, recv_sem=gq_recv,
        device_id=(s - 1, h), device_id_type=MESH,
    )

    lower = s * rows - prefix_ref[s]
    position = s * rows + lax.broadcasted_iota(jnp.int32, (rows, 1), 0)

    def attend(base, first):
        start = base * rows
        span = plane * rows
        keys = kv[pl.ds(pl.multiple_of(start, span), span), :head_width]
        values = kv[pl.ds(pl.multiple_of(start, span), span), head_width:]
        key_position = start + lax.broadcasted_iota(jnp.int32, (1, span), 1)
        allowed = key_position >= lower
        if first:
            allowed = allowed & (key_position <= position)
        for j in range(head_count):
            columns = slice(j * head_width, (j + 1) * head_width)
            scores = rows_by_rows(q_ref[:, columns], keys) * (head_width ** (-0.5) * log2_e)
            scores = jnp.where(allowed, scores, masked_score)
            top = jnp.max(scores, axis=1, keepdims=True)
            if not first:
                top = jnp.maximum(top, run_max[j])
                factor = jnp.exp2(run_max[j] - top)
            weights = jnp.exp2(scores - top)
            weighted = weights * rows_by_rows(g_ref[:, columns], values)
            part_sum = jnp.sum(weights, axis=1, keepdims=True)
            part_delta = jnp.sum(weighted, axis=1, keepdims=True)
            part_grad = jnp.dot(
                weighted.astype(jnp.bfloat16), keys, preferred_element_type=jnp.float32
            )
            part_key = jnp.dot(
                weights.astype(jnp.bfloat16), keys, preferred_element_type=jnp.float32
            )
            run_max[j] = top
            if first:
                run_sum[j] = part_sum
                run_delta[j] = part_delta
                total_grad[j] = part_grad
                total_key[j] = part_key
            else:
                run_sum[j] = run_sum[j] * factor + part_sum
                run_delta[j] = run_delta[j] * factor + part_delta
                total_grad[j] = total_grad[j] * factor + part_grad
                total_key[j] = total_key[j] * factor + part_key

    own = z * plane
    arrive(own + px)
    to_y(own + px).start()

    @pl.when(z < planes - 1)
    def _():
        to_z(own + px).start()

    @pl.when(s > 0)
    def _():
        d_copy.start()

    own_w.start()
    for step in range(1, heads):
        w_copy(step).start()
    arrive(own + py)

    def pass_far(distance, base):
        @pl.when((z < planes - 1) & (distance + 1 > near_planes))
        def _():
            to_z(base + py).start()
            to_z(base + pd).start()

    if near_planes == 0:
        @pl.when(z < planes - 1)
        def _():
            to_z(own + py).start()
    arrive(own + pd)
    if near_planes == 0:
        @pl.when(z < planes - 1)
        def _():
            to_z(own + pd).start()
    attend(own, True)

    def earlier_plane(distance, carry):
        base = (z - distance) * plane
        for column in (p, px):
            arrive(base + column)

            @pl.when(distance <= near_planes)
            def _():
                to_y(base + column).start()

            @pl.when(z < planes - 1)
            def _():
                to_z(base + column).start()

        arrive(base + py)
        arrive(base + pd)
        pass_far(distance, base)
        attend(base, False)
        return carry

    lax.fori_loop(1, z + 1, earlier_plane, 0)

    for j in range(head_count):
        inverse = 1.0 / run_sum[j]
        delta = run_delta[j] * inverse
        grad = (total_grad[j] - delta * total_key[j]) * (inverse * head_width ** (-0.5))
        mine[:, j * head_width:(j + 1) * head_width] = grad.astype(jnp.bfloat16)

    @pl.when(s > 0)
    def _():
        gq_copy.start()

    def fan_copy(step):
        return pltpu.make_async_remote_copy(
            src_ref=gq.at[h], dst_ref=gq.at[h], send_sem=fan_send.at[step],
            recv_sem=fan_recv.at[step], device_id=(s, (h + step) % heads), device_id_type=MESH,
        )

    def fan_arrive(step):
        sender = (h + heads - step) % heads
        pltpu.make_async_remote_copy(
            src_ref=gq.at[sender], dst_ref=gq.at[sender], send_sem=fan_send.at[step],
            recv_sem=fan_recv.at[step], device_id=(s, sender), device_id_type=MESH,
        ).wait_recv()

    own_w.wait()
    for step in range(1, heads):
        w_arrive(step)

    @pl.when(s < sections - 1)
    def _():
        gq_copy.wait_recv()
        for step in range(1, heads):
            fan_copy(step).start()
        d_copy.wait_recv()
        for step in range(1, heads):
            fan_arrive(step)
        tile = min(proj_tile, features)
        for t in range(features // tile):
            columns = slice(t * tile, (t + 1) * tile)
            hidden = din[:, columns].astype(jnp.float32)
            for group in range(heads):
                hidden = hidden + rows_by_rows(gq[group], wbuf[group, columns, :])
            out_ref[:, columns] = hidden.astype(jnp.bfloat16)
        for step in range(1, heads):
            fan_copy(step).wait_send()

    @pl.when(s == sections - 1)
    def _():
        out_ref[...] = jnp.zeros_like(out_ref)

    @pl.when(s > 0)
    def _():
        d_copy.wait_send()
        gq_copy.wait_send()

    for step in range(1, heads):
        w_copy(step).wait_send()
    to_x(s).wait_send()
    to_y(s).wait_send()
    to_y(own + px).wait_send()

    @pl.when(z < planes - 1)
    def _():
        to_z(s).wait_send()
        to_z(own + px).wait_send()
        if near_planes == 0:
            to_z(own + py).wait_send()
            to_z(own + pd).wait_send()

    def drain(distance, carry):
        base = (z - distance) * plane
        for column in (p, px):
            @pl.when(distance <= near_planes)
            def _():
                to_y(base + column).wait_send()

            @pl.when(z < planes - 1)
            def _():
                to_z(base + column).wait_send()

        @pl.when((z < planes - 1) & (distance + 1 > near_planes))
        def _():
            to_z(base + py).wait_send()
            to_z(base + pd).wait_send()

        return carry

    lax.fori_loop(1, z + 1, drain, 0)


def shards(queries, keys, values, d_attn, d_out, w_query, prefix_len):
    sections = lax.axis_size("section")
    heads = lax.axis_size("head")
    rows, head_width = keys.shape
    width = queries.shape[1]
    head_count = width // head_width
    features = d_out.shape[1]
    vmem = pl.BlockSpec(memory_space=pltpu.VMEM)
    anywhere = pl.BlockSpec(memory_space=pl.ANY)
    dma = pltpu.SemaphoreType.DMA
    return pl.pallas_call(
        functools.partial(kernel, sections, heads),
        out_shape=jax.ShapeDtypeStruct(d_out.shape, d_out.dtype),
        in_specs=[
            pl.BlockSpec(memory_space=pltpu.SMEM), vmem, vmem, vmem, vmem, anywhere, anywhere,
        ],
        out_specs=vmem,
        scratch_shapes=[
            pltpu.VMEM((sections * rows, 2 * head_width), jnp.bfloat16),
            pltpu.VMEM((rows, width), jnp.bfloat16),
            pltpu.VMEM((heads, rows, width), jnp.bfloat16),
            pltpu.VMEM((heads, features, width), jnp.bfloat16),
            pltpu.VMEM((rows, features), jnp.bfloat16),
            pltpu.VMEM((head_count, rows, 1), jnp.float32),
            pltpu.VMEM((head_count, rows, 1), jnp.float32),
            pltpu.VMEM((head_count, rows, 1), jnp.float32),
            pltpu.VMEM((head_count, rows, head_width), jnp.float32),
            pltpu.VMEM((head_count, rows, head_width), jnp.float32),
            dma((sections,)),
            dma((sections,)),
            dma((sections,)),
            dma((sections,)),
            dma((heads,)),
            dma((heads,)),
            dma,
            dma,
            dma,
            dma,
            dma,
            dma((heads,)),
            dma((heads,)),
        ],
        compiler_params=pltpu.CompilerParams(
            collective_id=0, has_side_effects=True, vmem_limit_bytes=40 * 1024 * 1024
        ),
    )(prefix_len, queries, keys, values, d_attn, d_out, w_query)


def solution(mesh):
    placed = (
        P("section", "head"),
        P("section", "head"),
        P("section", "head"),
        P("section", "head"),
        P("section", "head"),
        P(None, "head"),
        P(),
    )
    return jax.shard_map(
        shards, mesh=mesh, in_specs=placed, out_specs=P("section", "head"), check_vma=False
    )
```

time: 158 us -> 69.5 us (0.44); the launches traced: 155 us -> 69.2 us
  waiting for transfers between devices: 90.3 us -> 0 us
  Pallas kernels: 0 us -> 60.9 us
  matrix products: 36.2 us -> 0 us
  between operations: 14.2 us -> 0.02 us
  other arithmetic: 5.85 us -> 0 us
  local copies, waits for them, and re-layouts: 3.84 us -> 8.31 us
  starting transfers between devices: 4.02 us -> 0 us
    pallas_call x0 -> x1, Pallas kernels: none -> 60.9 us  [shards(): pl.pallas_call(functools.partial(kernel, sections, heads), out_shape=jax....]
    all_gather x1 -> x0, waiting for transfers between devices: 54.7 us -> none  [shards(): lax.all_gather(key_values, 'section', axis=0, tiled=True)]
    dot_general x21 -> x0, matrix products: 36.2 us -> none  [the longest x5 8.7 us: absorb(): jnp.dot(weights.astype(jnp.bfloat16), key_part, preferred_element_type=jn...]
    reduce_scatter x1 -> x0, waiting for transfers between devices: 18.8 us -> none  [shards(): lax.psum_scatter(lax.dot_general(w_query, grad_query, (((1,), (1,)), ((),...]
    ppermute x1 -> x0, waiting for transfers between devices: 16.8 us -> none  [shifted(): lax.ppermute(value, axis, [(source, source + steps) for source in range(f...]
    unnamed x5 -> x15, local copies, waits for them, and re-layouts: 0.89 us -> 8.31 us
    ppermute x1 -> x0, starting transfers between devices: 3.98 us -> none  [shifted(): lax.ppermute(value, axis, [(source, source + steps) for source in range(f...]
    reduce_sum x5 -> x0, other arithmetic: 2.51 us -> none  [absorb(): run_sum = run_sum * factor + jnp.sum(weights, axis=1)]
  transfers between devices with their start and end apart: 3 -> 0, of which waited for: 3 -> 0; matrix products, arithmetic and copies ran while one was open for 1% -> 0% of each run, Pallas kernels for 0% -> 0%
where the time goes in v1:
time: 69.5 us; the launch traced here: 69.2 us
  Pallas kernels  60.9 us (88%)
  local copies, waits for them, and re-layouts  8.31 us (12%)
    pallas_call x1, Pallas kernels, shards(): pl.pallas_call(functools.partial(kernel, sections, heads), out_shape=jax....  60.9 us
    unnamed x15, local copies, waits for them, and re-layouts  8.31 us

profile of v1, /device:TPU:25, one launch (start us, length us, event | category | flops | bytes accessed | tf_op | source)
XLA Modules:
  0.0 69.2 jit_solution(5962591728693402722)
XLA Ops:
  0.0 0.0 copy-start
  0.0 2.2 %copy-done = bf16[4096,512]{1,0:T(8,128)(2,1)S(1)} copy-done((bf16[4096,512]{1,0:T(8,128)(2,1)S(1)}, bf16[4096,512]{1,0:T(8,128)(2,1)}, u32[]{:S(2)}) %copy-start) | copy-done | bytes 4194328
  2.2 0.0 copy-start.1
  2.2 1.1 %copy-done.1 = bf16[192,2048]{1,0:T(8,128)(2,1)S(1)} copy-done((bf16[192,2048]{1,0:T(8,128)(2,1)S(1)}, bf16[192,2048]{1,0:T(8,128)(2,1)}, u32[]{:S(2)}) %copy-start.1) | copy-done | bytes 786456
  3.3 0.0 copy-start.2
  3.3 0.9 %copy-done.2 = bf16[192,512]{1,0:T(8,128)(2,1)S(1)} copy-done((bf16[192,512]{1,0:T(8,128)(2,1)S(1)}, bf16[192,512]{1,0:T(8,128)(2,1)}, u32[]{:S(2)}) %copy-start.2) | copy-done | bytes 196632
  4.2 0.0 copy-start.3
  4.3 0.9 %copy-done.3 = bf16[192,512]{1,0:T(8,128)(2,1)S(1)} copy-done((bf16[192,512]{1,0:T(8,128)(2,1)S(1)}, bf16[192,512]{1,0:T(8,128)(2,1)}, u32[]{:S(2)}) %copy-start.3) | copy-done | bytes 196632
  5.2 0.0 copy-start.4
  5.2 0.8 %copy-done.4 = bf16[192,128]{1,0:T(8,128)(2,1)S(1)} copy-done((bf16[192,128]{1,0:T(8,128)(2,1)S(1)}, bf16[192,128]{1,0:T(8,128)(2,1)}, u32[]{:S(2)}) %copy-start.4) | copy-done | bytes 49176
  6.0 0.0 copy-start.5
  6.0 0.8 %copy-done.5 = bf16[192,128]{1,0:T(8,128)(2,1)S(1)} copy-done((bf16[192,128]{1,0:T(8,128)(2,1)S(1)}, bf16[192,128]{1,0:T(8,128)(2,1)}, u32[]{:S(2)}) %copy-start.5) | copy-done | bytes 49176
  6.8 0.0 copy-start.6
  6.8 0.7 copy-done.6
  7.4 60.9 %shard_map.73 = bf16[192,2048]{1,0:T(8,128)(2,1)S(1)} custom-call(s32[16]{0:T(128)S(1)} %copy-done.6, bf16[192,512]{1,0:T(8,128)(2,1)S(1)} %copy-done.2, bf16[192,128]{1,0:T(8,128)(2,1)S(1)} %copy-done.4, bf16[192,128]{1,0:T(8,128)(2,1)S(1)} %copy-done.5, bf16[192,512]{1,0:T(8,128)(2,1)S(1)} %copy-done.3, bf16[192,2048]{1,0:T(8,128)(2,1)S(1)} %copy-done.1, ...), custom_call_target="tpu_custom_call" | custom-call | tf_op jit(solution)/shard_map/pallas_call | solution.py:333
  68.3 0.9 %copy.9 = bf16[192,2048]{1,0:T(8,128)(2,1)} copy(bf16[192,2048]{1,0:T(8,128)(2,1)S(1)} %shard_map.73) | data formatting | bytes 1572864
Async XLA Ops:
  0.0 2.2 %copy-start = (bf16[4096,512]{1,0:T(8,128)(2,1)S(1)}, bf16[4096,512]{1,0:T(8,128)(2,1)}, u32[]{:S(2)}) copy-start(bf16[4096,512]{1,0:T(8,128)(2,1)} %w_ref.1) | copy-start | bytes 12582916
  2.2 1.1 %copy-start.1 = (bf16[192,2048]{1,0:T(8,128)(2,1)S(1)}, bf16[192,2048]{1,0:T(8,128)(2,1)}, u32[]{:S(2)}) copy-start(bf16[192,2048]{1,0:T(8,128)(2,1)} %dout_ref.1) | copy-start | bytes 2359300
  3.3 0.9 %copy-start.2 = (bf16[192,512]{1,0:T(8,128)(2,1)S(1)}, bf16[192,512]{1,0:T(8,128)(2,1)}, u32[]{:S(2)}) copy-start(bf16[192,512]{1,0:T(8,128)(2,1)} %q_ref.1) | copy-start | bytes 589828
  4.2 0.9 %copy-start.3 = (bf16[192,512]{1,0:T(8,128)(2,1)S(1)}, bf16[192,512]{1,0:T(8,128)(2,1)}, u32[]{:S(2)}) copy-start(bf16[192,512]{1,0:T(8,128)(2,1)} %g_ref.1) | copy-start | bytes 589828
  5.2 0.8 %copy-start.4 = (bf16[192,128]{1,0:T(8,128)(2,1)S(1)}, bf16[192,128]{1,0:T(8,128)(2,1)}, u32[]{:S(2)}) copy-start(bf16[192,128]{1,0:T(8,128)(2,1)} %k_ref.1) | copy-start | bytes 147460
  6.0 0.8 %copy-start.5 = (bf16[192,128]{1,0:T(8,128)(2,1)S(1)}, bf16[192,128]{1,0:T(8,128)(2,1)}, u32[]{:S(2)}) copy-start(bf16[192,128]{1,0:T(8,128)(2,1)} %v_ref.1) | copy-start | bytes 147460
  6.8 0.7 copy-start.6

commit v2 on v1

--- a/solution.py
+++ b/solution.py
@@ -11,7 +11,8 @@
 masked_score = -1e30
 log2_e = 1.4426950408889634
 plane = 4
-near_planes = 2
+near_left = 2
+near_right = 0
 proj_tile = 512
 
 
@@ -22,15 +23,15 @@
 
 
 def kernel(
-    sections, heads, prefix_ref, q_ref, k_ref, v_ref, g_ref, dout_ref, w_ref, out_ref,
-    kv, mine, gq, wbuf, din, run_max, run_sum, run_delta, total_grad, total_key,
+    sections, heads, prefix_ref, q_hbm, k_ref, v_ref, g_hbm, dout_ref, w_ref, out_ref,
+    q_ref, g_ref, local_sem, partial, out_block, out_sem, kv, mine, gq, wbuf, din, run_max, run_sum, run_delta, total_grad, total_key,
     kv_recv, x_send, y_send, z_send, w_send, w_recv, w_local, d_send, d_recv,
     gq_send, gq_recv, fan_send, fan_recv,
 ):
     s = lax.axis_index("section")
     h = lax.axis_index("head")
     rows, head_width = k_ref.shape
-    head_count = q_ref.shape[1] // head_width
+    head_count = q_hbm.shape[1] // head_width
     features = dout_ref.shape[1]
     planes = sections // plane
     z = s // plane
@@ -41,6 +42,7 @@
     py = p + 2 - 4 * y
     pd = px + 2 - 4 * y
     x_side = z * plane + px
+    near = near_left * (1 - x) + near_right * x
     y_side = z * plane + py
 
     def block(b):
@@ -94,8 +96,17 @@
     def _():
         greet(s - 1, h)
 
-    kv[pl.ds(pl.multiple_of(s * rows, rows), rows), :head_width] = k_ref[...]
-    kv[pl.ds(pl.multiple_of(s * rows, rows), rows), head_width:] = v_ref[...]
+    own_rows = pl.ds(pl.multiple_of(s * rows, rows), rows)
+    loads = [
+        pltpu.make_async_copy(k_ref, kv.at[own_rows, :head_width], local_sem.at[0]),
+        pltpu.make_async_copy(v_ref, kv.at[own_rows, head_width:], local_sem.at[1]),
+        pltpu.make_async_copy(q_hbm, q_ref, local_sem.at[2]),
+        pltpu.make_async_copy(g_hbm, g_ref, local_sem.at[3]),
+    ]
+    for load in loads:
+        load.start()
+    loads[0].wait()
+    loads[1].wait()
     pl.semaphore_wait(barrier, 1 + heads + up + down + after + before)
 
     to_x(s).start()
@@ -129,15 +140,23 @@
         src_ref=dout_ref, dst_ref=din, send_sem=d_send, recv_sem=d_recv,
         device_id=(s - 1, h), device_id_type=MESH,
     )
-    gq_copy = pltpu.make_async_remote_copy(
-        src_ref=mine, dst_ref=gq.at[h], send_sem=gq_send, recv_sem=gq_recv,
-        device_id=(s - 1, h), device_id_type=MESH,
-    )
+
+    def gq_copy(j):
+        return pltpu.make_async_remote_copy(
+            src_ref=mine.at[j], dst_ref=gq.at[h, j], send_sem=gq_send.at[j],
+            recv_sem=gq_recv.at[j], device_id=(s - 1, h), device_id_type=MESH,
+        )
+
+    def finish(j):
+        inverse = 1.0 / run_sum[j]
+        delta = run_delta[j] * inverse
+        grad = (total_grad[j] - delta * total_key[j]) * (inverse * head_width ** (-0.5))
+        mine[j] = grad.astype(jnp.bfloat16)
 
     lower = s * rows - prefix_ref[s]
     position = s * rows + lax.broadcasted_iota(jnp.int32, (rows, 1), 0)
 
-    def attend(base, first):
+    def attend(base, first, last=False):
         start = base * rows
         span = plane * rows
         keys = kv[pl.ds(pl.multiple_of(start, span), span), :head_width]
@@ -175,6 +194,9 @@
                 run_delta[j] = run_delta[j] * factor + part_delta
                 total_grad[j] = total_grad[j] * factor + part_grad
                 total_key[j] = total_key[j] * factor + part_key
+            if last:
+                finish(j)
+                gq_copy(j).start()
 
     own = z * plane
     arrive(own + px)
@@ -183,10 +205,6 @@
     @pl.when(z < planes - 1)
     def _():
         to_z(own + px).start()
-
-    @pl.when(s > 0)
-    def _():
-        d_copy.start()
 
     own_w.start()
     for step in range(1, heads):
@@ -194,28 +212,28 @@
     arrive(own + py)
 
     def pass_far(distance, base):
-        @pl.when((z < planes - 1) & (distance + 1 > near_planes))
+        @pl.when((z < planes - 1) & (distance + 1 > near))
         def _():
             to_z(base + py).start()
             to_z(base + pd).start()
 
-    if near_planes == 0:
-        @pl.when(z < planes - 1)
-        def _():
-            to_z(own + py).start()
     arrive(own + pd)
-    if near_planes == 0:
-        @pl.when(z < planes - 1)
-        def _():
-            to_z(own + pd).start()
+    pass_far(0, own)
+
+    @pl.when(s > 0)
+    def _():
+        d_copy.start()
+
+    loads[2].wait()
+    loads[3].wait()
     attend(own, True)
 
-    def earlier_plane(distance, carry):
+    def earlier_plane(distance):
         base = (z - distance) * plane
         for column in (p, px):
             arrive(base + column)
 
-            @pl.when(distance <= near_planes)
+            @pl.when(distance <= near)
             def _():
                 to_y(base + column).start()
 
@@ -226,64 +244,100 @@
         arrive(base + py)
         arrive(base + pd)
         pass_far(distance, base)
-        attend(base, False)
+
+    def middle_plane(distance, carry):
+        earlier_plane(distance)
+        attend((z - distance) * plane, False)
         return carry
 
-    lax.fori_loop(1, z + 1, earlier_plane, 0)
-
-    for j in range(head_count):
-        inverse = 1.0 / run_sum[j]
-        delta = run_delta[j] * inverse
-        grad = (total_grad[j] - delta * total_key[j]) * (inverse * head_width ** (-0.5))
-        mine[:, j * head_width:(j + 1) * head_width] = grad.astype(jnp.bfloat16)
-
-    @pl.when(s > 0)
-    def _():
-        gq_copy.start()
-
-    def fan_copy(step):
+    lax.fori_loop(1, z, middle_plane, 0)
+
+    @pl.when(z > 0)
+    def _():
+        earlier_plane(z)
+        attend(0, False, True)
+
+    @pl.when(z == 0)
+    def _():
+        for j in range(head_count):
+            finish(j)
+
+    @pl.when((z == 0) & (s > 0))
+    def _():
+        for j in range(head_count):
+            gq_copy(j).start()
+
+    def fan_copy(step, j):
         return pltpu.make_async_remote_copy(
-            src_ref=gq.at[h], dst_ref=gq.at[h], send_sem=fan_send.at[step],
-            recv_sem=fan_recv.at[step], device_id=(s, (h + step) % heads), device_id_type=MESH,
+            src_ref=gq.at[h, j], dst_ref=gq.at[h, j], send_sem=fan_send.at[step, j],
+            recv_sem=fan_recv.at[step, j], device_id=(s, (h + step) % heads), device_id_type=MESH,
         )
 
-    def fan_arrive(step):
+    def fan_arrive(step, j):
         sender = (h + heads - step) % heads
         pltpu.make_async_remote_copy(
-            src_ref=gq.at[sender], dst_ref=gq.at[sender], send_sem=fan_send.at[step],
-            recv_sem=fan_recv.at[step], device_id=(s, sender), device_id_type=MESH,
+            src_ref=gq.at[sender, j], dst_ref=gq.at[sender, j], send_sem=fan_send.at[step, j],
+            recv_sem=fan_recv.at[step, j], device_id=(s, sender), device_id_type=MESH,
         ).wait_recv()
 
     own_w.wait()
     for step in range(1, heads):
         w_arrive(step)
 
+    tile = min(proj_tile, features)
+    tiles = [slice(t * tile, (t + 1) * tile) for t in range(features // tile)]
+
+    def out_copy(t):
+        return pltpu.make_async_copy(out_block.at[:, tiles[t]], out_ref.at[:, tiles[t]], out_sem.at[t])
+
     @pl.when(s < sections - 1)
     def _():
-        gq_copy.wait_recv()
-        for step in range(1, heads):
-            fan_copy(step).start()
-        d_copy.wait_recv()
-        for step in range(1, heads):
-            fan_arrive(step)
-        tile = min(proj_tile, features)
-        for t in range(features // tile):
-            columns = slice(t * tile, (t + 1) * tile)
-            hidden = din[:, columns].astype(jnp.float32)
-            for group in range(heads):
-                hidden = hidden + rows_by_rows(gq[group], wbuf[group, columns, :])
-            out_ref[:, columns] = hidden.astype(jnp.bfloat16)
-        for step in range(1, heads):
-            fan_copy(step).wait_send()
+        cut = max(head_count // 2, 1)
+        parts = [range(i, min(i + cut, head_count)) for i in range(0, head_count, cut)]
+        for index, part in enumerate(parts):
+            for j in part:
+                gq_copy(j).wait_recv()
+                for step in range(1, heads):
+                    fan_copy(step, j).start()
+            if index == 0:
+                d_copy.wait_recv()
+            for j in part:
+                for step in range(1, heads):
+                    fan_arrive(step, j)
+            channels = slice(part[0] * head_width, (part[-1] + 1) * head_width)
+            grads = [
+                jnp.concatenate([gq[group, j] for j in part], axis=1) for group in range(heads)
+            ]
+            for t, columns in enumerate(tiles):
+                if index == 0:
+                    hidden = din[:, columns].astype(jnp.float32)
+                else:
+                    hidden = partial[:, columns]
+                for group in range(heads):
+                    hidden = hidden + rows_by_rows(grads[group], wbuf[group, columns, channels])
+                if index < len(parts) - 1:
+                    partial[:, columns] = hidden
+                else:
+                    out_block[:, columns] = hidden.astype(jnp.bfloat16)
+                    out_copy(t).start()
+        for j in range(head_count):
+            for step in range(1, heads):
+                fan_copy(step, j).wait_send()
 
     @pl.when(s == sections - 1)
     def _():
-        out_ref[...] = jnp.zeros_like(out_ref)
+        out_block[...] = jnp.zeros_like(out_block)
+        for t in range(len(tiles)):
+            out_copy(t).start()
+
+    for t in range(len(tiles)):
+        out_copy(t).wait()
 
     @pl.when(s > 0)
     def _():
         d_copy.wait_send()
-        gq_copy.wait_send()
+        for j in range(head_count):
+            gq_copy(j).wait_send()
 
     for step in range(1, heads):
         w_copy(step).wait_send()
@@ -295,14 +349,16 @@
     def _():
         to_z(s).wait_send()
         to_z(own + px).wait_send()
-        if near_planes == 0:
-            to_z(own + py).wait_send()
-            to_z(own + pd).wait_send()
+
+    @pl.when((z < planes - 1) & (near < 1))
+    def _():
+        to_z(own + py).wait_send()
+        to_z(own + pd).wait_send()
 
     def drain(distance, carry):
         base = (z - distance) * plane
         for column in (p, px):
-            @pl.when(distance <= near_planes)
+            @pl.when(distance <= near)
             def _():
                 to_y(base + column).wait_send()
 
@@ -310,7 +366,7 @@
             def _():
                 to_z(base + column).wait_send()
 
-        @pl.when((z < planes - 1) & (distance + 1 > near_planes))
+        @pl.when((z < planes - 1) & (distance + 1 > near))
         def _():
             to_z(base + py).wait_send()
             to_z(base + pd).wait_send()
@@ -327,20 +383,26 @@
     width = queries.shape[1]
     head_count = width // head_width
     features = d_out.shape[1]
-    vmem = pl.BlockSpec(memory_space=pltpu.VMEM)
     anywhere = pl.BlockSpec(memory_space=pl.ANY)
     dma = pltpu.SemaphoreType.DMA
     return pl.pallas_call(
         functools.partial(kernel, sections, heads),
         out_shape=jax.ShapeDtypeStruct(d_out.shape, d_out.dtype),
         in_specs=[
-            pl.BlockSpec(memory_space=pltpu.SMEM), vmem, vmem, vmem, vmem, anywhere, anywhere,
+            pl.BlockSpec(memory_space=pltpu.SMEM), anywhere, anywhere, anywhere, anywhere,
+            anywhere, anywhere,
         ],
-        out_specs=vmem,
+        out_specs=anywhere,
         scratch_shapes=[
+            pltpu.VMEM((rows, width), jnp.bfloat16),
+            pltpu.VMEM((rows, width), jnp.bfloat16),
+            dma((4,)),
+            pltpu.VMEM((rows, features), jnp.float32),
+            pltpu.VMEM((rows, features), jnp.bfloat16),
+            dma((max(1, features // min(proj_tile, features)),)),
             pltpu.VMEM((sections * rows, 2 * head_width), jnp.bfloat16),
-            pltpu.VMEM((rows, width), jnp.bfloat16),
-            pltpu.VMEM((heads, rows, width), jnp.bfloat16),
+            pltpu.VMEM((head_count, rows, head_width), jnp.bfloat16),
+            pltpu.VMEM((heads, head_count, rows, head_width), jnp.bfloat16),
             pltpu.VMEM((heads, features, width), jnp.bfloat16),
             pltpu.VMEM((rows, features), jnp.bfloat16),
             pltpu.VMEM((head_count, rows, 1), jnp.float32),
@@ -357,13 +419,13 @@
             dma,
             dma,
             dma,
-            dma,
-            dma,
-            dma((heads,)),
-            dma((heads,)),
+            dma((head_count,)),
+            dma((head_count,)),
+            dma((heads, head_count)),
+            dma((heads, head_count)),
         ],
         compiler_params=pltpu.CompilerParams(
-            collective_id=0, has_side_effects=True, vmem_limit_bytes=40 * 1024 * 1024
+            collective_id=0, has_side_effects=True, vmem_limit_bytes=62 * 1024 * 1024
         ),
     )(prefix_len, queries, keys, values, d_attn, d_out, w_query)
 

time: 69.5 us -> 43.1 us (0.62)
  Pallas kernels: 60.9 us -> 40.8 us
  local copies, waits for them, and re-layouts: 8.31 us -> 2.09 us
    pallas_call x1, Pallas kernels: 60.9 us -> 40.8 us  [shards(): pl.pallas_call(functools.partial(kernel, sections, heads), out_shape=jax....]
    unnamed x15 -> x1, local copies, waits for them, and re-layouts: 8.31 us -> 2.09 us
where the time goes in v2:
time: 43.1 us; the launch traced here: 42.9 us
  Pallas kernels  40.8 us (95%)
  local copies, waits for them, and re-layouts  2.09 us (5%)
    pallas_call x1, Pallas kernels, shards(): pl.pallas_call(functools.partial(kernel, sections, heads), out_shape=jax....  40.8 us
    unnamed x1, local copies, waits for them, and re-layouts  2.09 us

profile of v2, /device:TPU:25, one launch (start us, length us, event | category | flops | bytes accessed | tf_op | source)
XLA Modules:
  0.0 42.9 jit_solution(9131072375531882828)
XLA Ops:
  0.0 40.8 %shard_map.73 = bf16[192,2048]{1,0:T(8,128)(2,1)} custom-call(s32[16]{0:T(128)} %prefix_ref.1, bf16[192,512]{1,0:T(8,128)(2,1)} %q_hbm.1, bf16[192,128]{1,0:T(8,128)(2,1)} %k_ref.1, bf16[192,128]{1,0:T(8,128)(2,1)} %v_ref.1, bf16[192,512]{1,0:T(8,128)(2,1)} %g_hbm.1, bf16[192,2048]{1,0:T(8,128)(2,1)} %dout_ref.1, bf16[4096,512]{1,0:T(8,128)(2,1)} %w_ref.1), custom_call_target="tpu_custom_call" | custom-call | tf_op jit(solution)/shard_map/pallas_call | solution.py:388
  40.8 2.1 %copy.9 = bf16[192,2048]{1,0:T(8,128)(2,1)} copy(bf16[192,2048]{1,0:T(8,128)(2,1)} %shard_map.73) | data formatting | bytes 1572864
